TPU v7x, 512 devices: a whole 4x8x8 slice. The times are simulated.
512 devices in a mesh: brick: 128 (over y, z, core), ch: 4 (over x).
Axes of the slice: x: 4, y: 8, z: 8, core: 2. Of those that a mesh axis runs over, the one named last changes fastest.
Arguments:
- features: bfloat16 [256, 16384], P('ch', 'brick'), may hold values from -6 to 6
- owner_map: int32 [16384, 1], P('brick'), may hold values from 0 to 127; in each aligned block of 128 rows (0 to 127, 128 to 255, ...) at most 2 rows name the same one
- kernel_map: int32 [27, 32768], P(None, 'brick'), may hold values from 0 to 320, as said below
- send_lists: int32 [2, 4096], P(None, 'brick'), may hold values from 0 to 255
- drop_first: int32 [256, 32768], P('ch', 'brick'), may hold values 0 or 1
- drop_second: int32 [256, 32768], P('ch', 'brick'), may hold values 0 or 1
- weight_first: bfloat16 [27, 256, 256], P(None, 'ch'), may hold values from -0.15625 to 0.15625
- weight_second: bfloat16 [27, 256, 256], P(None, 'ch'), may hold values from -0.15625 to 0.15625
- cotangent: bfloat16 [256, 32768], P('ch', 'brick'), may hold values from -24 to 24
Outputs:
- block_out: bfloat16 [256, 32768], P('ch', 'brick')
- grad_features: bfloat16 [256, 16384], P('ch', 'brick')
- grad_weight_first: bfloat16 [27, 256, 256], P(None, 'ch')
- grad_weight_second: bfloat16 [27, 256, 256], P(None, 'ch')
Inputs may be any that keep to these rules, and one draw needn't show every extreme that they name: `owner_map`: among the rows of one scan group, at most 2 are owned by the same brick. `kernel_map`: column 320 means that the neighbour is absent; in the middle offset row, slot i of every brick names column 32 + i.
All inputs are finite; a program needn't handle non-finite values. No bound on the sum of `drop_first` or of `drop_second` on one device may be relied on, other than what follows from the above.
Results may differ from a plain program's by a relative error of at most 0.0064.
Values may be sent and summed in bfloat16 or wider, within the bound.
A program may use at most 64 MiB of HBM per device.

v0:
```python
import jax
import jax.numpy as jnp
from jax import lax
from jax.sharding import PartitionSpec as P

KEEP_RATE = 0.9


def with_halo(block, sides, width):
    for axis, dim in sides:
        count = lax.axis_size(axis)
        forward = [(i, i + 1) for i in range(count - 1)]
        backward = [(target, source) for source, target in forward]
        low = lax.ppermute(
            lax.slice_in_dim(block, block.shape[dim] - width, None, axis=dim), axis, forward
        )
        high = lax.ppermute(lax.slice_in_dim(block, 0, width, axis=dim), axis, backward)
        block = jnp.concatenate([low, block, high], axis=dim)
    return block


def slope_silu(value):
    sig = jax.nn.sigmoid(value)
    return sig * (1.0 + value * (1.0 - sig))


def spread(field, send_lists):
    rim_width = send_lists.shape[1]
    outgoing = jnp.concatenate(
        [jnp.take(field, send_lists[0], axis=1), jnp.take(field, send_lists[1], axis=1)], axis=1
    )
    padded = with_halo(outgoing, (("brick", 1),), rim_width)
    return jnp.concatenate([padded[:, :rim_width], field, padded[:, 3 * rim_width :]], axis=1)


def convolve(extended, kernel_map, weight):
    gathered = jnp.take(extended, kernel_map, axis=1, mode="fill", fill_value=0)
    return (
        lax.psum_scatter(
            jnp.einsum("ckr,kco->or", gathered, weight, preferred_element_type=jnp.float32),
            "ch",
            scatter_dimension=0,
            tiled=True,
        ),
        gathered,
    )


def adjoint(gathered, kernel_map, grad_local, weight, extent):
    gathered_grad = lax.all_gather(grad_local, "ch", axis=0, tiled=True)
    weight_grad = jnp.einsum(
        "ckr,or->kco", gathered, gathered_grad, preferred_element_type=jnp.float32
    )
    pushed = jnp.einsum("kco,or->ckr", weight, gathered_grad, preferred_element_type=jnp.float32)
    returned = (
        jnp.zeros((pushed.shape[0], extent), jnp.float32).at[:, kernel_map].add(pushed, mode="drop")
    )
    return (weight_grad, returned)


def fold_back(returned, send_lists, slot_count):
    rim_width = send_lists.shape[1]
    borders = jnp.concatenate(
        [returned[:, :rim_width], returned[:, rim_width + slot_count :]], axis=1
    )
    padded = with_halo(borders, (("brick", 1),), rim_width)
    interior = returned[:, rim_width : rim_width + slot_count]
    interior = interior.at[:, send_lists[0]].add(padded[:, :rim_width])
    return interior.at[:, send_lists[1]].add(padded[:, 3 * rim_width :])


def local(
    features,
    owner_map,
    kernel_map,
    send_lists,
    drop_first,
    drop_second,
    weight_first,
    weight_second,
    cotangent,
):
    bricks = lax.axis_size("brick")
    channels = features.shape[0]
    slot_count = 2 * features.shape[1]
    capacity = slot_count // bricks
    targets = owner_map[:, 0]
    matches = (targets[:, None] == jnp.arange(bricks, dtype=jnp.int32)[None, :]).astype(jnp.int32)
    running = jnp.cumsum(matches, axis=0)
    ordinal = jnp.sum((running - 1) * matches, axis=1)
    columns = targets * capacity + ordinal
    outgoing = jnp.zeros((channels, slot_count), features.dtype).at[:, columns].set(features)
    tallies = jnp.sum(matches, axis=0)[None, :].astype(jnp.bfloat16)
    arrived, arrived_tallies = (
        lax.all_to_all(
            outgoing.reshape(channels, bricks, capacity),
            "brick",
            split_axis=1,
            concat_axis=1,
            tiled=True,
        ),
        lax.all_to_all(tallies, "brick", split_axis=1, concat_axis=1, tiled=True),
    )
    voxels = arrived.reshape(channels, slot_count)
    occupied = (
        jnp.arange(capacity, dtype=jnp.int32)[None, :]
        < arrived_tallies[0].astype(jnp.int32)[:, None]
    )
    occupied = occupied.reshape(slot_count).astype(jnp.float32)
    keep_first = occupied[None, :] * drop_first.astype(jnp.float32) / KEEP_RATE
    keep_second = occupied[None, :] * drop_second.astype(jnp.float32) / KEEP_RATE
    extended_voxels = spread(voxels, send_lists)
    extent = extended_voxels.shape[1]
    conv_first, gathered_voxels = convolve(extended_voxels, kernel_map, weight_first)
    hidden = (jax.nn.silu(conv_first) * keep_first).astype(jnp.bfloat16)
    extended_hidden = spread(hidden, send_lists)
    conv_second, gathered_hidden = convolve(extended_hidden, kernel_map, weight_second)
    summed = voxels.astype(jnp.float32) + keep_second * conv_second
    block_out = jax.nn.silu(summed).astype(jnp.bfloat16)
    grad_pre = cotangent.astype(jnp.float32) * slope_silu(summed)
    grad_second = (grad_pre * keep_second).astype(jnp.bfloat16)
    weight_grad_second, returned_second = adjoint(
        gathered_hidden, kernel_map, grad_second, weight_second, extent
    )
    grad_hidden = fold_back(returned_second, send_lists, slot_count)
    grad_first = (grad_hidden * keep_first * slope_silu(conv_first)).astype(jnp.bfloat16)
    weight_grad_first, returned_first = adjoint(
        gathered_voxels, kernel_map, grad_first, weight_first, extent
    )
    weight_grad_first, weight_grad_second = lax.psum(
        (weight_grad_first, weight_grad_second), "brick"
    )
    grad_voxels = (grad_pre + fold_back(returned_first, send_lists, slot_count)).astype(
        jnp.bfloat16
    )
    homeward = lax.all_to_all(
        grad_voxels.reshape(channels, bricks, capacity),
        "brick",
        split_axis=1,
        concat_axis=1,
        tiled=True,
    )
    grad_features = jnp.take(homeward.reshape(channels, slot_count), columns, axis=1)
    factor = float(bricks * slot_count) ** (-0.5)
    return (
        block_out,
        grad_features,
        (weight_grad_first * factor).astype(jnp.bfloat16),
        (weight_grad_second * factor).astype(jnp.bfloat16),
    )


def solution(mesh):
    return jax.shard_map(
        local,
        mesh=mesh,
        in_specs=(
            P("ch", "brick"),
            P("brick", None),
            P(None, "brick"),
            P(None, "brick"),
            P("ch", "brick"),
            P("ch", "brick"),
            P(None, "ch", None),
            P(None, "ch", None),
            P("ch", "brick"),
        ),
        out_specs=(P("ch", "brick"), P("ch", "brick"), P(None, "ch", None), P(None, "ch", None)),
        check_vma=False,
    )
```

profile of v0, /device:TPU:24, one launch (start us, length us, event | category | flops | bytes accessed | tf_op | source)
XLA Modules:
  0.0 440.2 jit_solution(2850545359836102251)
XLA Ops:
  8.2 1.4 fusion.20
  11.7 1.5 scatter_custom_fusion
  13.1 17.3 %all-to-all-start = ((bf16[64,128,2]{0,2,1:T(2,128)(2,1)}), bf16[64,128,2]{0,2,1:T(2,128)(2,1)S(1)}, u32[]{:S(2)}, u32[]{:S(2)}) async-start(bf16[64,128,2]{0,2,1:T(2,128)(2,1)} %bitcast.4), calls=%async_computation | async-start | bytes 131072 | tf_op jit(solution)/shard_map/all_to_all | solution.py:95
  32.9 6.8 %all-to-all-done = bf16[64,128,2]{0,2,1:T(2,128)(2,1)S(1)} async-done(((bf16[64,128,2]{0,2,1:T(2,128)(2,1)}), bf16[64,128,2]{0,2,1:T(2,128)(2,1)S(1)}, u32[]{:S(2)}, u32[]{:S(2)}) %all-to-all-start) | async-done | bytes 32800 | tf_op jit(solution)/shard_map/all_to_all | solution.py:95
  40.4 1.9 collective-permute-start
  43.0 5.7 %collective-permute-start.1 = (bf16[64,32]{0,1:T(8,128)(2,1)S(1)}, bf16[64,32]{0,1:T(8,128)(2,1)S(1)}, u32[]{:S(2)}, u32[]{:S(2)}) collective-permute-start(bf16[64,32]{0,1:T(8,128)(2,1)S(1)} %select_bitcast_fusion.3), channel_id=1, source_target_pairs={{4,0},{8,4},{12,8},{16,12},{20,16},{24,20},{28,24},{32,28},{36,32}... | collective-permute-start | bytes 12296 | tf_op jit(solution)/shard_map/ppermute | solution.py:17
  50.1 13.0 %gather_fusion.3 = bf16[6912,64]{1,0:T(8,128)(2,1)S(1)} fusion(bf16[64,320]{0,1:T(8,128)(2,1)S(1)} %pad_maximum_fusion, s32[7168]{0:T(1024)S(1)} %pad_clamp_fusion), kind=kCustom, calls=%fused_computation.1.clone | custom fusion | bytes 1797120 | tf_op jit(solution)/shard_map/jit(_take)/gather | solution.py:37
  64.1 2.0 convolution_bitcast_fusion.5
  67.2 19.5 %all_to_all.16 = bf16[1,128,1]{2,0,1:T(2,128)(2,1)S(1)} all-to-all(bf16[1,128,1]{2,0,1:T(2,128)(2,1)S(1)} %copy.100), channel_id=1, replica_groups=mesh['brick'=128,'ch'=4] {'brick'}, dimensions={1} | all-to-all | bytes 512 | tf_op jit(solution)/shard_map/all_to_all | solution.py:102
  86.7 2.4 convert_reduce_fusion
  93.0 1.9 collective-permute-start.2
  95.1 5.8 %collective-permute-start.3 = (bf16[64,32]{1,0:T(8,128)(2,1)S(1)}, bf16[64,32]{1,0:T(8,128)(2,1)S(1)}, u32[]{:S(2)}, u32[]{:S(2)}) collective-permute-start(bf16[64,32]{1,0:T(8,128)(2,1)S(1)} %select_bitcast_fusion.1), channel_id=1, source_target_pairs={{4,0},{8,4},{12,8},{16,12},{20,16},{24,20},{28,24},{32,28},{36,32}... | collective-permute-start | bytes 12296 | tf_op jit(solution)/shard_map/ppermute | solution.py:17
  100.9 1.4 collective-permute-done.3
  102.5 13.0 %gather_fusion.6 = bf16[6912,64]{1,0:T(8,128)(2,1)S(1)} fusion(bf16[64,320]{0,1:T(8,128)(2,1)S(1)} %copy.108, s32[7168]{0:T(1024)S(1)} %copy-done.7), kind=kCustom, calls=%fused_computation.5.clone | custom fusion | bytes 1797120 | tf_op jit(solution)/shard_map/jit(_take)/gather | solution.py:37
  118.5 24.4 %reduce-scatter.9.cloned.1.call-done = f32[64,256]{1,0:T(8,128)} async-done(((f32[256,256]{1,0:T(8,128)}), f32[64,256]{1,0:T(8,128)}) %reduce-scatter.9.cloned.1.call-update) | async-done | bytes 65552 | tf_op jit(solution)/shard_map/reduce_scatter | solution.py:39
  143.9 12.2 %all_gather.6 = bf16[256,256]{1,0:T(8,128)(2,1)S(1)} all-gather(bf16[64,256]{1,0:T(8,128)(2,1)S(1)} %multiply_convert_fusion.3), channel_id=1, replica_groups=mesh['brick'=128,'ch'=4] {'ch'}, dimensions={0}, use_global_device_ids=true | all-gather | bytes 163840 | tf_op jit(solution)/shard_map/all_gather | solution.py:50
  157.1 2.5 copy.120
  159.6 39.1 %scatter_custom_fusion.1 = f32[64,320]{0,1:T(8,128)S(1)} fusion(s32[6912]{0:T(1024)} %copy-done.18, f32[6912,64]{1,0:T(8,128)} %bitcast.101, f32[]{:T(128)} %constant.44.clone.1), kind=kCustom, calls=%fused_computation.40 | custom fusion | flops 442368 | bytes 82432 | tf_op jit(solution)/shard_map/scatter-add | solution.py:56
  198.7 1.9 collective-permute-start.4
  200.6 5.9 %collective-permute-start.5 = (f32[64,32]{0,1:T(8,128)S(1)}, f32[64,32]{0,1:T(8,128)S(1)}, u32[]{:S(2)}, u32[]{:S(2)}) collective-permute-start(f32[64,32]{0,1:T(8,128)S(1)} %get-tuple-element.44), channel_id=1, source_target_pairs={{4,0},{8,4},{12,8},{16,12},{20,16},{24,20},{28,24},{32,28},{36,32}... | collective-permute-start | bytes 24584 | tf_op jit(solution)/shard_map/ppermute | solution.py:17
  206.5 2.6 convolution_bitcast_fusion
  211.0 12.0 %all_gather.7 = bf16[256,256]{1,0:T(8,128)(2,1)S(1)} all-gather(bf16[64,256]{1,0:T(8,128)(2,1)S(1)} %multiply_convert_fusion.2), channel_id=1, replica_groups=mesh['brick'=128,'ch'=4] {'ch'}, dimensions={0}, use_global_device_ids=true | all-gather | bytes 163840 | tf_op jit(solution)/shard_map/all_gather | solution.py:50
  223.0 1.7 convolution_bitcast_fusion.1
  224.7 1.6 convolution_bitcast_fusion.2
  226.3 2.5 copy.121
  228.8 39.1 %scatter_custom_fusion.4 = f32[64,320]{0,1:T(8,128)S(1)} fusion(s32[6912]{0:T(1024)} %copy-done.18, f32[6912,64]{1,0:T(8,128)} %bitcast.100, f32[]{:T(128)} %constant.44.clone.1), kind=kCustom, calls=%fused_computation.38 | custom fusion | flops 442368 | bytes 82432 | tf_op jit(solution)/shard_map/scatter-add | solution.py:56
  268.0 1.9 collective-permute-start.6
  269.9 5.8 %collective-permute-start.7 = (f32[64,32]{0,1:T(8,128)S(1)}, f32[64,32]{0,1:T(8,128)S(1)}, u32[]{:S(2)}, u32[]{:S(2)}) collective-permute-start(f32[64,32]{0,1:T(8,128)S(1)} %get-tuple-element.42), channel_id=1, source_target_pairs={{4,0},{8,4},{12,8},{16,12},{20,16},{24,20},{28,24},{32,28},{36,32}... | collective-permute-start | bytes 24584 | tf_op jit(solution)/shard_map/ppermute | solution.py:17
  278.9 13.2 %all-to-all-start.2 = ((bf16[64,128,2]{0,2,1:T(2,128)(2,1)}), bf16[64,128,2]{0,2,1:T(2,128)(2,1)S(1)}, u32[]{:S(2)}, u32[]{:S(2)}) async-start(bf16[64,128,2]{0,2,1:T(2,128)(2,1)} %bitcast.36), calls=%async_computation.2 | async-start | bytes 131072 | tf_op jit(solution)/shard_map/all_to_all | solution.py:136
  292.2 9.2 %all-to-all-done.2 = bf16[64,128,2]{0,2,1:T(2,128)(2,1)S(1)} async-done(((bf16[64,128,2]{0,2,1:T(2,128)(2,1)}), bf16[64,128,2]{0,2,1:T(2,128)(2,1)S(1)}, u32[]{:S(2)}, u32[]{:S(2)}) %all-to-all-start.2) | async-done | bytes 32800 | tf_op jit(solution)/shard_map/all_to_all | solution.py:136
  302.9 127.1 %all-reduce.3.cloned.1.call-done = (f32[27,64,256]{2,1,0:T(8,128)}, f32[27,64,256]{2,1,0:T(8,128)}) async-done(((f32[27,64,256]{2,1,0:T(8,128)}, f32[27,64,256]{2,1,0:T(8,128)}), (f32[27,64,256]{2,1,0:T(8,128)}, f32[27,64,256]{2,1,0:T(8,128)})) %all-reduce.3.cloned.1.call-update) | async-done | bytes 3538960 | tf_op jit(solution)/shard_map/psum | solution.py:130
  429.9 3.7 multiply_convert_fusion
  (129 shorter events, 25.9 us)
Async XLA Ops:
  7.2 109.3 %copy-start = (bf16[27,64,256]{2,1,0:T(8,128)(2,1)S(1)}, bf16[27,64,256]{2,1,0:T(8,128)(2,1)}, u32[]{:S(2)}) copy-start(bf16[27,64,256]{2,1,0:T(8,128)(2,1)} %param.20) | copy-start | bytes 2654212
  13.1 26.6 %all-to-all-start = ((bf16[64,128,2]{0,2,1:T(2,128)(2,1)}), bf16[64,128,2]{0,2,1:T(2,128)(2,1)S(1)}, u32[]{:S(2)}, u32[]{:S(2)}) async-start(bf16[64,128,2]{0,2,1:T(2,128)(2,1)} %bitcast.4), calls=%async_computation | async-start | bytes 131072 | tf_op jit(solution)/shard_map/all_to_all | solution.py:95
  30.5 60.1 %reduce-scatter.7.cloned.1.call-start = ((), (), s32[]{:S(2)}) async-start(), calls=%async_computation.5 | async-start | bytes 327680 | tf_op jit(solution)/shard_map/reduce_scatter | solution.py:39
  32.9 17.2 %copy-start.20 = (pred[32]{0:T(512)(128)(4,1)}, pred[32]{0:T(512)(128)(4,1)S(1)}, u32[]{:S(2)}) copy-start(pred[32]{0:T(512)(128)(4,1)S(1)} %get-tuple-element.48) | copy-start | bytes 100
  32.9 17.2 %copy-start.22 = (pred[32]{0:T(512)(128)(4,1)}, pred[32]{0:T(512)(128)(4,1)S(1)}, u32[]{:S(2)}) copy-start(pred[32]{0:T(512)(128)(4,1)S(1)} %get-tuple-element.36) | copy-start | bytes 100
  32.9 17.2 %copy-start.18 = (s32[6912]{0:T(1024)}, s32[6912]{0:T(1024)S(1)}, u32[]{:S(2)}) copy-start(s32[6912]{0:T(1024)S(1)} %reshape.262) | copy-start | bytes 82948
  32.9 30.3 %copy-start.19 = (s32[1024]{0:T(1024)}, s32[1024]{0:T(1024)S(1)}, u32[]{:S(2)}) copy-start(s32[1024]{0:T(1024)S(1)} %pad_clamp_fusion.2) | copy-start | bytes 12292
  40.4 8.4 %collective-permute-start = (bf16[64,32]{0,1:T(8,128)(2,1)S(1)}, bf16[64,32]{0,1:T(8,128)(2,1)S(1)}, u32[]{:S(2)}, u32[]{:S(2)}) collective-permute-start(bf16[64,32]{0,1:T(8,128)(2,1)S(1)} %select_bitcast_fusion.4), channel_id=1, source_target_pairs={{0,4},{4,8},{8,12},{12,16},{16,20},{20,24},{24,28},{28,32},{32,36}... | collective-permute-start | bytes 12296 | tf_op jit(solution)/shard_map/ppermute | solution.py:14
  43.0 7.1 %collective-permute-start.1 = (bf16[64,32]{0,1:T(8,128)(2,1)S(1)}, bf16[64,32]{0,1:T(8,128)(2,1)S(1)}, u32[]{:S(2)}, u32[]{:S(2)}) collective-permute-start(bf16[64,32]{0,1:T(8,128)(2,1)S(1)} %select_bitcast_fusion.3), channel_id=1, source_target_pairs={{4,0},{8,4},{12,8},{16,12},{20,16},{24,20},{28,24},{32,28},{36,32}... | collective-permute-start | bytes 12296 | tf_op jit(solution)/shard_map/ppermute | solution.py:17
  64.1 26.5 %copy-start.10 = (s32[64,256]{1,0:T(8,128)S(1)}, s32[64,256]{1,0:T(8,128)}, u32[]{:S(2)}) copy-start(s32[64,256]{1,0:T(8,128)} %param.17) | copy-start | bytes 196612
  66.1 26.9 %copy-start.23 = (pred[32]{0:T(512)(128)(4,1)S(1)}, pred[32]{0:T(512)(128)(4,1)}, u32[]{:S(2)}) copy-start(pred[32]{0:T(512)(128)(4,1)} %copy-done.22) | copy-start | bytes 100
  66.1 29.0 %copy-start.21 = (pred[32]{0:T(512)(128)(4,1)S(1)}, pred[32]{0:T(512)(128)(4,1)}, u32[]{:S(2)}) copy-start(pred[32]{0:T(512)(128)(4,1)} %copy-done.20) | copy-start | bytes 100
  66.1 36.4 %copy-start.7 = (s32[7168]{0:T(1024)S(1)}, s32[7168]{0:T(1024)}, u32[]{:S(2)}) copy-start(s32[7168]{0:T(1024)} %copy-done.6) | copy-start | bytes 86020
  67.0 76.0 %reduce-scatter.9.cloned.1.call-start = ((), (), s32[]{:S(2)}) async-start(), calls=%async_computation.6 | async-start | bytes 327680 | tf_op jit(solution)/shard_map/reduce_scatter | solution.py:39
  93.0 7.8 %collective-permute-start.2 = (bf16[64,32]{1,0:T(8,128)(2,1)S(1)}, bf16[64,32]{1,0:T(8,128)(2,1)S(1)}, u32[]{:S(2)}, u32[]{:S(2)}) collective-permute-start(bf16[64,32]{1,0:T(8,128)(2,1)S(1)} %select_bitcast_fusion.2), channel_id=1, source_target_pairs={{0,4},{4,8},{8,12},{12,16},{16,20},{20,24},{24,28},{28,32},{32,36}... | collective-permute-start | bytes 12296 | tf_op jit(solution)/shard_map/ppermute | solution.py:14
  95.1 7.2 %collective-permute-start.3 = (bf16[64,32]{1,0:T(8,128)(2,1)S(1)}, bf16[64,32]{1,0:T(8,128)(2,1)S(1)}, u32[]{:S(2)}, u32[]{:S(2)}) collective-permute-start(bf16[64,32]{1,0:T(8,128)(2,1)S(1)} %select_bitcast_fusion.1), channel_id=1, source_target_pairs={{4,0},{8,4},{12,8},{16,12},{20,16},{24,20},{28,24},{32,28},{36,32}... | collective-permute-start | bytes 12296 | tf_op jit(solution)/shard_map/ppermute | solution.py:17
  116.4 26.5 %copy-start.13 = (s32[64,256]{1,0:T(8,128)S(1)}, s32[64,256]{1,0:T(8,128)}, u32[]{:S(2)}) copy-start(s32[64,256]{1,0:T(8,128)} %param.18) | copy-start | bytes 196612
  116.5 26.5 %copy-start.16 = (bf16[64,256]{1,0:T(8,128)(2,1)S(1)}, bf16[64,256]{1,0:T(8,128)(2,1)}, u32[]{:S(2)}) copy-start(bf16[64,256]{1,0:T(8,128)(2,1)} %param.21) | copy-start | bytes 98308
  117.8 312.1 %all-reduce.3.cloned.1.call-start = ((), (), s32[]{:S(2)}) async-start(), calls=%async_computation.7 | async-start | bytes 7077888 | tf_op jit(solution)/shard_map/psum | solution.py:130
  118.5 25.4 %copy-start.8 = (bf16[64,256]{1,0:T(8,128)(2,1)}, bf16[64,256]{1,0:T(8,128)(2,1)S(1)}, u32[]{:S(2)}) copy-start(bf16[64,256]{1,0:T(8,128)(2,1)S(1)} %copy.99) | copy-start | bytes 98308
  198.7 10.4 %collective-permute-start.4 = (f32[64,32]{0,1:T(8,128)S(1)}, f32[64,32]{0,1:T(8,128)S(1)}, u32[]{:S(2)}, u32[]{:S(2)}) collective-permute-start(f32[64,32]{0,1:T(8,128)S(1)} %get-tuple-element.45), channel_id=1, source_target_pairs={{0,4},{4,8},{8,12},{12,16},{16,20},{20,24},{24,28},{28,32},{32,36}... | collective-permute-start | bytes 24584 | tf_op jit(solution)/shard_map/ppermute | solution.py:14
  200.6 22.4 %copy-start.2 = (bf16[27,256,64]{1,2,0:T(8,128)(2,1)S(1)}, bf16[27,256,64]{1,2,0:T(8,128)(2,1)}, u32[]{:S(2)}) copy-start(bf16[27,256,64]{1,2,0:T(8,128)(2,1)} %copy-done.1) | copy-start | bytes 2654212
  200.6 9.4 %collective-permute-start.5 = (f32[64,32]{0,1:T(8,128)S(1)}, f32[64,32]{0,1:T(8,128)S(1)}, u32[]{:S(2)}, u32[]{:S(2)}) collective-permute-start(f32[64,32]{0,1:T(8,128)S(1)} %get-tuple-element.44), channel_id=1, source_target_pairs={{4,0},{8,4},{12,8},{16,12},{20,16},{24,20},{28,24},{32,28},{36,32}... | collective-permute-start | bytes 24584 | tf_op jit(solution)/shard_map/ppermute | solution.py:17
  226.3 49.4 %copy-start.9 = (bf16[64,256]{1,0:T(8,128)(2,1)S(1)}, bf16[64,256]{1,0:T(8,128)(2,1)}, u32[]{:S(2)}) copy-start(bf16[64,256]{1,0:T(8,128)(2,1)} %copy-done.8) | copy-start | bytes 98308
  226.3 49.4 %copy-start.14 = (s32[64,256]{1,0:T(8,128)S(1)}, s32[64,256]{1,0:T(8,128)}, u32[]{:S(2)}) copy-start(s32[64,256]{1,0:T(8,128)} %param.18) | copy-start | bytes 196612
  226.3 49.4 %copy-start.15 = (f32[64,256]{1,0:T(8,128)S(1)}, f32[64,256]{1,0:T(8,128)}, u32[]{:S(2)}) copy-start(f32[64,256]{1,0:T(8,128)} %reduce-scatter.9.cloned.1.call-done) | copy-start | bytes 196612
  226.3 49.4 %copy-start.17 = (bf16[64,256]{1,0:T(8,128)(2,1)S(1)}, bf16[64,256]{1,0:T(8,128)(2,1)}, u32[]{:S(2)}) copy-start(bf16[64,256]{1,0:T(8,128)(2,1)} %param.21) | copy-start | bytes 98308
  228.8 63.4 %copy-start.27 = (s32[128,1]{0,1:T(1,128)S(1)}, s32[128,1]{0,1:T(1,128)}, u32[]{:S(2)}) copy-start(s32[128,1]{0,1:T(1,128)} %copy-done.26) | copy-start | bytes 1540
  228.8 73.3 %copy-start.25 = (pred[128]{0:T(512)(128)(4,1)S(1)}, pred[128]{0:T(512)(128)(4,1)}, u32[]{:S(2)}) copy-start(pred[128]{0:T(512)(128)(4,1)} %get-tuple-element.34) | copy-start | bytes 388
  268.0 8.5 %collective-permute-start.6 = (f32[64,32]{0,1:T(8,128)S(1)}, f32[64,32]{0,1:T(8,128)S(1)}, u32[]{:S(2)}, u32[]{:S(2)}) collective-permute-start(f32[64,32]{0,1:T(8,128)S(1)} %get-tuple-element.43), channel_id=1, source_target_pairs={{0,4},{4,8},{8,12},{12,16},{16,20},{20,24},{24,28},{28,32},{32,36}... | collective-permute-start | bytes 24584 | tf_op jit(solution)/shard_map/ppermute | solution.py:14
  269.9 7.5 %collective-permute-start.7 = (f32[64,32]{0,1:T(8,128)S(1)}, f32[64,32]{0,1:T(8,128)S(1)}, u32[]{:S(2)}, u32[]{:S(2)}) collective-permute-start(f32[64,32]{0,1:T(8,128)S(1)} %get-tuple-element.42), channel_id=1, source_target_pairs={{4,0},{8,4},{12,8},{16,12},{20,16},{24,20},{28,24},{32,28},{36,32}... | collective-permute-start | bytes 24584 | tf_op jit(solution)/shard_map/ppermute | solution.py:17
  278.9 22.4 %all-to-all-start.2 = ((bf16[64,128,2]{0,2,1:T(2,128)(2,1)}), bf16[64,128,2]{0,2,1:T(2,128)(2,1)S(1)}, u32[]{:S(2)}, u32[]{:S(2)}) async-start(bf16[64,128,2]{0,2,1:T(2,128)(2,1)} %bitcast.36), calls=%async_computation.2 | async-start | bytes 131072 | tf_op jit(solution)/shard_map/all_to_all | solution.py:136
  (10 other events, 56.9 us)
Sparse Core Ops, SparseCore 0:
  67.1 23.4 reduce-scatter.6
  117.9 24.9 reduce-scatter.8
  224.8 205.0 all-reduce.2
where the time goes:
time: 441 us; the launch traced here: 440 us
  waiting for transfers between devices  172 us (39%)
  other arithmetic  97.8 us (22%)
  starting transfers between devices  61.5 us (14%)
  blocking collectives  43.7 us (10%)
  local copies, waits for them, and re-layouts  42.5 us (10%)
  between operations  14.5 us (3%)
  matrix products  8.64 us (2%)
    psum x1, waiting for transfers between devices, local(): lax.psum((weight_grad_first, weight_grad_second), 'brick')  127 us
    scatter-add x2, other arithmetic, adjoint(): jnp.zeros((pushed.shape[0], extent), jnp.float32).at[:, kernel_map]  78.2 us
    gather x4, local copies, waits for them, and re-layouts, convolve(): gathered = jnp.take(extended, kernel_map, axis=1, mode='fill', fill_value=0)  27.8 us
    reduce_scatter x2, waiting for transfers between devices, convolve(): lax.psum_scatter(jnp.einsum('ckr,kco->or', gathered, weight, preferred_el...  25.8 us
    all_gather x2, blocking collectives, adjoint(): gathered_grad = lax.all_gather(grad_local, 'ch', axis=0, tiled=True)  24.2 us
    ppermute x4, starting transfers between devices, with_halo(): lax.ppermute(lax.slice_in_dim(block, 0, width, axis=dim), axis, backward)  23.1 us
    all_to_all x1, blocking collectives, local(): lax.all_to_all(tallies, 'brick', split_axis=1, concat_axis=1, tiled=True)  19.5 us
    all_to_all x1, starting transfers between devices, local(): lax.all_to_all(outgoing.reshape(channels, bricks, capacity), 'brick', spl...  17.3 us
  transfers between devices with their start and end apart: 13, of which 7 were waited for; matrix products, arithmetic and copies ran while one was open for 13% of the time, Pallas kernels for 0%

commit v1 on v0

--- a/solution.py
+++ b/solution.py
@@ -47,7 +47,9 @@
 
 
 def adjoint(gathered, kernel_map, grad_local, weight, extent):
-    gathered_grad = lax.all_gather(grad_local, "ch", axis=0, tiled=True)
+    gathered_grad = jnp.concatenate(
+        lax.all_to_all(jnp.stack([grad_local] * lax.axis_size("ch")), "ch", 0, 0), axis=0
+    )
     weight_grad = jnp.einsum(
         "ckr,or->kco", gathered, gathered_grad, preferred_element_type=jnp.float32
     )

time: 441 us -> 434 us (0.984)
  blocking collectives: 43.7 us -> 28 us
    all_gather x2 -> x0, blocking collectives: 24.2 us -> none  [adjoint(): gathered_grad = lax.all_gather(grad_local, 'ch', axis=0, tiled=True)]
    all_to_all x0 -> x1, blocking collectives: none -> 8.5 us  [adjoint(): lax.all_to_all(jnp.stack([grad_local] * lax.axis_size('ch')), 'ch', 0, 0)]
  transfers between devices with their start and end apart: 13 -> 14, of which waited for: 7 -> 9; matrix products, arithmetic and copies ran while one was open for 13% -> 13% of each run, Pallas kernels for 0% -> 0%
where the time goes in v1:
time: 434 us; the launch traced here: 433 us
  waiting for transfers between devices  176 us (41%)
  other arithmetic  97.9 us (23%)
  starting transfers between devices  64.8 us (15%)
  local copies, waits for them, and re-layouts  43.2 us (10%)
  blocking collectives  28 us (6%)
  between operations  14.5 us (3%)
  matrix products  8.62 us (2%)
    psum x1, waiting for transfers between devices, local(): lax.psum((weight_grad_first, weight_grad_second), 'brick')  127 us
    scatter-add x2, other arithmetic, adjoint(): jnp.zeros((pushed.shape[0], extent), jnp.float32).at[:, kernel_map]  78.2 us
    gather x4, local copies, waits for them, and re-layouts, convolve(): gathered = jnp.take(extended, kernel_map, axis=1, mode='fill', fill_value=0)  27.8 us
    reduce_scatter x2, waiting for transfers between devices, convolve(): lax.psum_scatter(jnp.einsum('ckr,kco->or', gathered, weight, preferred_el...  26.4 us
    ppermute x4, starting transfers between devices, with_halo(): lax.ppermute(lax.slice_in_dim(block, 0, width, axis=dim), axis, backward)  23 us
    all_to_all x1, blocking collectives, local(): lax.all_to_all(tallies, 'brick', split_axis=1, concat_axis=1, tiled=True)  19.5 us
    all_to_all x1, starting transfers between devices, local(): lax.all_to_all(outgoing.reshape(channels, bricks, capacity), 'brick', spl...  17.3 us
    all_to_all x1, starting transfers between devices, local(): lax.all_to_all(grad_voxels.reshape(channels, bricks, capacity), 'brick',...  13.4 us
  transfers between devices with their start and end apart: 14, of which 9 were waited for; matrix products, arithmetic and copies ran while one was open for 13% of the time, Pallas kernels for 0%

profile of v1, /device:TPU:24, one launch (start us, length us, event | category | flops | bytes accessed | tf_op | source)
XLA Modules:
  0.0 432.8 jit_solution(11263075319558506086)
XLA Ops:
  11.6 1.5 scatter_custom_fusion
  13.1 17.3 %all-to-all-start = ((bf16[64,128,2]{0,2,1:T(2,128)(2,1)}), bf16[64,128,2]{0,2,1:T(2,128)(2,1)S(1)}, u32[]{:S(2)}, u32[]{:S(2)}) async-start(bf16[64,128,2]{0,2,1:T(2,128)(2,1)} %bitcast.4), calls=%async_computation | async-start | bytes 131072 | tf_op jit(solution)/shard_map/all_to_all | solution.py:97
  32.9 6.8 %all-to-all-done = bf16[64,128,2]{0,2,1:T(2,128)(2,1)S(1)} async-done(((bf16[64,128,2]{0,2,1:T(2,128)(2,1)}), bf16[64,128,2]{0,2,1:T(2,128)(2,1)S(1)}, u32[]{:S(2)}, u32[]{:S(2)}) %all-to-all-start) | async-done | bytes 32800 | tf_op jit(solution)/shard_map/all_to_all | solution.py:97
  40.4 1.9 collective-permute-start
  43.0 5.7 %collective-permute-start.1 = (bf16[64,32]{0,1:T(8,128)(2,1)S(1)}, bf16[64,32]{0,1:T(8,128)(2,1)S(1)}, u32[]{:S(2)}, u32[]{:S(2)}) collective-permute-start(bf16[64,32]{0,1:T(8,128)(2,1)S(1)} %select_bitcast_fusion.3), channel_id=1, source_target_pairs={{4,0},{8,4},{12,8},{16,12},{20,16},{24,20},{28,24},{32,28},{36,32}... | collective-permute-start | bytes 12296 | tf_op jit(solution)/shard_map/ppermute | solution.py:17
  50.1 13.0 %gather_fusion.3 = bf16[6912,64]{1,0:T(8,128)(2,1)S(1)} fusion(bf16[64,320]{0,1:T(8,128)(2,1)S(1)} %pad_maximum_fusion, s32[7168]{0:T(1024)S(1)} %pad_clamp_fusion), kind=kCustom, calls=%fused_computation.1.clone | custom fusion | bytes 1797120 | tf_op jit(solution)/shard_map/jit(_take)/gather | solution.py:37
  64.1 2.0 convolution_bitcast_fusion.5
  67.2 19.5 %all_to_all.26 = bf16[1,128,1]{2,0,1:T(2,128)(2,1)S(1)} all-to-all(bf16[1,128,1]{2,0,1:T(2,128)(2,1)S(1)} %copy.96), channel_id=1, replica_groups=mesh['brick'=128,'ch'=4] {'brick'}, dimensions={1} | all-to-all | bytes 512 | tf_op jit(solution)/shard_map/all_to_all | solution.py:104
  86.7 2.4 convert_reduce_fusion
  93.0 1.9 collective-permute-start.2
  95.1 5.8 %collective-permute-start.3 = (bf16[64,32]{1,0:T(8,128)(2,1)S(1)}, bf16[64,32]{1,0:T(8,128)(2,1)S(1)}, u32[]{:S(2)}, u32[]{:S(2)}) collective-permute-start(bf16[64,32]{1,0:T(8,128)(2,1)S(1)} %select_bitcast_fusion.1), channel_id=1, source_target_pairs={{4,0},{8,4},{12,8},{16,12},{20,16},{24,20},{28,24},{32,28},{36,32}... | collective-permute-start | bytes 12296 | tf_op jit(solution)/shard_map/ppermute | solution.py:17
  100.8 1.4 collective-permute-done.3
  102.5 13.0 %gather_fusion.6 = bf16[6912,64]{1,0:T(8,128)(2,1)S(1)} fusion(bf16[64,320]{0,1:T(8,128)(2,1)S(1)} %copy.104, s32[7168]{0:T(1024)S(1)} %copy-done.7), kind=kCustom, calls=%fused_computation.5.clone | custom fusion | bytes 1797120 | tf_op jit(solution)/shard_map/jit(_take)/gather | solution.py:37
  117.9 25.0 %reduce-scatter.9.cloned.1.call-done = f32[64,256]{1,0:T(8,128)} async-done(((f32[256,256]{1,0:T(8,128)}), f32[64,256]{1,0:T(8,128)}) %reduce-scatter.9.cloned.1.call-update) | async-done | bytes 65552 | tf_op jit(solution)/shard_map/reduce_scatter | solution.py:39
  143.9 8.5 %all_to_all.27 = bf16[4,64,256]{2,1,0:T(8,128)(2,1)S(1)} all-to-all(bf16[4,64,256]{2,1,0:T(8,128)(2,1)S(1)} %stack.4), channel_id=1, replica_groups=mesh['brick'=128,'ch'=4] {'ch'}, dimensions={0} | all-to-all | bytes 262144 | tf_op jit(solution)/shard_map/all_to_all | solution.py:51
  153.4 2.5 copy.116
  155.9 39.1 %scatter_custom_fusion.1 = f32[64,320]{0,1:T(8,128)S(1)} fusion(s32[6912]{0:T(1024)} %copy-done.16, f32[6912,64]{1,0:T(8,128)} %bitcast.101, f32[]{:T(128)} %constant.44.clone.1), kind=kCustom, calls=%fused_computation.36 | custom fusion | flops 442368 | bytes 82432 | tf_op jit(solution)/shard_map/scatter-add | solution.py:58
  195.0 1.9 collective-permute-start.4
  196.9 5.8 %collective-permute-start.5 = (f32[64,32]{0,1:T(8,128)S(1)}, f32[64,32]{0,1:T(8,128)S(1)}, u32[]{:S(2)}, u32[]{:S(2)}) collective-permute-start(f32[64,32]{0,1:T(8,128)S(1)} %get-tuple-element.44), channel_id=1, source_target_pairs={{4,0},{8,4},{12,8},{16,12},{20,16},{24,20},{28,24},{32,28},{36,32}... | collective-permute-start | bytes 24584 | tf_op jit(solution)/shard_map/ppermute | solution.py:17
  206.7 3.3 all-to-all-start.3
  210.0 2.6 convolution_bitcast_fusion
  212.6 3.3 all-to-all-done.3
  215.9 1.6 convolution_bitcast_fusion.1
  217.6 1.6 convolution_bitcast_fusion.2
  219.2 2.5 copy.117
  221.7 39.1 %scatter_custom_fusion.4 = f32[64,320]{0,1:T(8,128)S(1)} fusion(s32[6912]{0:T(1024)} %copy-done.16, f32[6912,64]{1,0:T(8,128)} %bitcast.100, f32[]{:T(128)} %constant.44.clone.1), kind=kCustom, calls=%fused_computation.34 | custom fusion | flops 442368 | bytes 82432 | tf_op jit(solution)/shard_map/scatter-add | solution.py:58
  260.9 1.9 collective-permute-start.6
  262.8 5.8 %collective-permute-start.7 = (f32[64,32]{0,1:T(8,128)S(1)}, f32[64,32]{0,1:T(8,128)S(1)}, u32[]{:S(2)}, u32[]{:S(2)}) collective-permute-start(f32[64,32]{0,1:T(8,128)S(1)} %get-tuple-element.42), channel_id=1, source_target_pairs={{4,0},{8,4},{12,8},{16,12},{20,16},{24,20},{28,24},{32,28},{36,32}... | collective-permute-start | bytes 24584 | tf_op jit(solution)/shard_map/ppermute | solution.py:17
  271.7 13.4 %all-to-all-start.4 = ((bf16[64,128,2]{0,2,1:T(2,128)(2,1)}), bf16[64,128,2]{0,2,1:T(2,128)(2,1)S(1)}, u32[]{:S(2)}, u32[]{:S(2)}) async-start(bf16[64,128,2]{0,2,1:T(2,128)(2,1)} %bitcast.38), calls=%async_computation.4 | async-start | bytes 131072 | tf_op jit(solution)/shard_map/all_to_all | solution.py:138
  285.1 9.2 %all-to-all-done.4 = bf16[64,128,2]{0,2,1:T(2,128)(2,1)S(1)} async-done(((bf16[64,128,2]{0,2,1:T(2,128)(2,1)}), bf16[64,128,2]{0,2,1:T(2,128)(2,1)S(1)}, u32[]{:S(2)}, u32[]{:S(2)}) %all-to-all-start.4) | async-done | bytes 32800 | tf_op jit(solution)/shard_map/all_to_all | solution.py:138
  295.8 126.7 %all-reduce.3.cloned.1.call-done = (f32[27,64,256]{2,1,0:T(8,128)}, f32[27,64,256]{2,1,0:T(8,128)}) async-done(((f32[27,64,256]{2,1,0:T(8,128)}, f32[27,64,256]{2,1,0:T(8,128)}), (f32[27,64,256]{2,1,0:T(8,128)}, f32[27,64,256]{2,1,0:T(8,128)})) %all-reduce.3.cloned.1.call-update) | async-done | bytes 3538960 | tf_op jit(solution)/shard_map/psum | solution.py:132
  422.5 3.7 multiply_convert_fusion
  (128 shorter events, 28.6 us)
Async XLA Ops:
  7.2 109.2 %copy-start = (bf16[27,64,256]{2,1,0:T(8,128)(2,1)S(1)}, bf16[27,64,256]{2,1,0:T(8,128)(2,1)}, u32[]{:S(2)}) copy-start(bf16[27,64,256]{2,1,0:T(8,128)(2,1)} %param.20) | copy-start | bytes 2654212
  13.1 26.6 %all-to-all-start = ((bf16[64,128,2]{0,2,1:T(2,128)(2,1)}), bf16[64,128,2]{0,2,1:T(2,128)(2,1)S(1)}, u32[]{:S(2)}, u32[]{:S(2)}) async-start(bf16[64,128,2]{0,2,1:T(2,128)(2,1)} %bitcast.4), calls=%async_computation | async-start | bytes 131072 | tf_op jit(solution)/shard_map/all_to_all | solution.py:97
  30.5 60.1 %reduce-scatter.7.cloned.1.call-start = ((), (), s32[]{:S(2)}) async-start(), calls=%async_computation.7 | async-start | bytes 327680 | tf_op jit(solution)/shard_map/reduce_scatter | solution.py:39
  32.8 17.2 %copy-start.18 = (pred[32]{0:T(512)(128)(4,1)}, pred[32]{0:T(512)(128)(4,1)S(1)}, u32[]{:S(2)}) copy-start(pred[32]{0:T(512)(128)(4,1)S(1)} %get-tuple-element.48) | copy-start | bytes 100
  32.8 17.2 %copy-start.20 = (pred[32]{0:T(512)(128)(4,1)}, pred[32]{0:T(512)(128)(4,1)S(1)}, u32[]{:S(2)}) copy-start(pred[32]{0:T(512)(128)(4,1)S(1)} %get-tuple-element.36) | copy-start | bytes 100
  32.9 30.3 %copy-start.17 = (s32[1024]{0:T(1024)}, s32[1024]{0:T(1024)S(1)}, u32[]{:S(2)}) copy-start(s32[1024]{0:T(1024)S(1)} %pad_clamp_fusion.2) | copy-start | bytes 12292
  40.4 8.4 %collective-permute-start = (bf16[64,32]{0,1:T(8,128)(2,1)S(1)}, bf16[64,32]{0,1:T(8,128)(2,1)S(1)}, u32[]{:S(2)}, u32[]{:S(2)}) collective-permute-start(bf16[64,32]{0,1:T(8,128)(2,1)S(1)} %select_bitcast_fusion.4), channel_id=1, source_target_pairs={{0,4},{4,8},{8,12},{12,16},{16,20},{20,24},{24,28},{28,32},{32,36}... | collective-permute-start | bytes 12296 | tf_op jit(solution)/shard_map/ppermute | solution.py:14
  43.0 7.1 %collective-permute-start.1 = (bf16[64,32]{0,1:T(8,128)(2,1)S(1)}, bf16[64,32]{0,1:T(8,128)(2,1)S(1)}, u32[]{:S(2)}, u32[]{:S(2)}) collective-permute-start(bf16[64,32]{0,1:T(8,128)(2,1)S(1)} %select_bitcast_fusion.3), channel_id=1, source_target_pairs={{4,0},{8,4},{12,8},{16,12},{20,16},{24,20},{28,24},{32,28},{36,32}... | collective-permute-start | bytes 12296 | tf_op jit(solution)/shard_map/ppermute | solution.py:17
  64.1 26.5 %copy-start.10 = (s32[64,256]{1,0:T(8,128)S(1)}, s32[64,256]{1,0:T(8,128)}, u32[]{:S(2)}) copy-start(s32[64,256]{1,0:T(8,128)} %param.17) | copy-start | bytes 196612
  66.1 26.9 %copy-start.21 = (pred[32]{0:T(512)(128)(4,1)S(1)}, pred[32]{0:T(512)(128)(4,1)}, u32[]{:S(2)}) copy-start(pred[32]{0:T(512)(128)(4,1)} %copy-done.20) | copy-start | bytes 100
  66.1 29.0 %copy-start.19 = (pred[32]{0:T(512)(128)(4,1)S(1)}, pred[32]{0:T(512)(128)(4,1)}, u32[]{:S(2)}) copy-start(pred[32]{0:T(512)(128)(4,1)} %copy-done.18) | copy-start | bytes 100
  66.1 36.4 %copy-start.7 = (s32[7168]{0:T(1024)S(1)}, s32[7168]{0:T(1024)}, u32[]{:S(2)}) copy-start(s32[7168]{0:T(1024)} %copy-done.6) | copy-start | bytes 86020
  67.0 76.0 %reduce-scatter.9.cloned.1.call-start = ((), (), s32[]{:S(2)}) async-start(), calls=%async_computation.8 | async-start | bytes 327680 | tf_op jit(solution)/shard_map/reduce_scatter | solution.py:39
  93.0 7.8 %collective-permute-start.2 = (bf16[64,32]{1,0:T(8,128)(2,1)S(1)}, bf16[64,32]{1,0:T(8,128)(2,1)S(1)}, u32[]{:S(2)}, u32[]{:S(2)}) collective-permute-start(bf16[64,32]{1,0:T(8,128)(2,1)S(1)} %select_bitcast_fusion.2), channel_id=1, source_target_pairs={{0,4},{4,8},{8,12},{12,16},{16,20},{20,24},{24,28},{28,32},{32,36}... | collective-permute-start | bytes 12296 | tf_op jit(solution)/shard_map/ppermute | solution.py:14
  95.1 7.2 %collective-permute-start.3 = (bf16[64,32]{1,0:T(8,128)(2,1)S(1)}, bf16[64,32]{1,0:T(8,128)(2,1)S(1)}, u32[]{:S(2)}, u32[]{:S(2)}) collective-permute-start(bf16[64,32]{1,0:T(8,128)(2,1)S(1)} %select_bitcast_fusion.1), channel_id=1, source_target_pairs={{4,0},{8,4},{12,8},{16,12},{20,16},{24,20},{28,24},{32,28},{36,32}... | collective-permute-start | bytes 12296 | tf_op jit(solution)/shard_map/ppermute | solution.py:17
  116.4 26.5 %copy-start.11 = (s32[64,256]{1,0:T(8,128)S(1)}, s32[64,256]{1,0:T(8,128)}, u32[]{:S(2)}) copy-start(s32[64,256]{1,0:T(8,128)} %param.18) | copy-start | bytes 196612
  116.4 26.5 %copy-start.14 = (bf16[64,256]{1,0:T(8,128)(2,1)S(1)}, bf16[64,256]{1,0:T(8,128)(2,1)}, u32[]{:S(2)}) copy-start(bf16[64,256]{1,0:T(8,128)(2,1)} %param.21) | copy-start | bytes 98308
  117.9 34.5 %copy-start.8 = (bf16[64,256]{1,0:T(8,128)(2,1)}, bf16[64,256]{1,0:T(8,128)(2,1)S(1)}, u32[]{:S(2)}) copy-start(bf16[64,256]{1,0:T(8,128)(2,1)S(1)} %copy.95) | copy-start | bytes 98308
  153.4 49.3 %copy-start.22 = (s32[2,32]{1,0:T(2,128)S(1)}, s32[2,32]{1,0:T(2,128)}, u32[]{:S(2)}) copy-start(s32[2,32]{1,0:T(2,128)} %param.16) | copy-start | bytes 772
  195.0 7.7 %collective-permute-start.4 = (f32[64,32]{0,1:T(8,128)S(1)}, f32[64,32]{0,1:T(8,128)S(1)}, u32[]{:S(2)}, u32[]{:S(2)}) collective-permute-start(f32[64,32]{0,1:T(8,128)S(1)} %get-tuple-element.45), channel_id=1, source_target_pairs={{0,4},{4,8},{8,12},{12,16},{16,20},{20,24},{24,28},{28,32},{32,36}... | collective-permute-start | bytes 24584 | tf_op jit(solution)/shard_map/ppermute | solution.py:14
  196.9 7.2 %collective-permute-start.5 = (f32[64,32]{0,1:T(8,128)S(1)}, f32[64,32]{0,1:T(8,128)S(1)}, u32[]{:S(2)}, u32[]{:S(2)}) collective-permute-start(f32[64,32]{0,1:T(8,128)S(1)} %get-tuple-element.44), channel_id=1, source_target_pairs={{4,0},{8,4},{12,8},{16,12},{20,16},{24,20},{28,24},{32,28},{36,32}... | collective-permute-start | bytes 24584 | tf_op jit(solution)/shard_map/ppermute | solution.py:17
  206.7 9.3 %all-to-all-start.3 = ((bf16[4,64,256]{2,1,0:T(8,128)(2,1)}), bf16[4,64,256]{2,1,0:T(8,128)(2,1)S(1)}, u32[]{:S(2)}, u32[]{:S(2)}) async-start(bf16[4,64,256]{2,1,0:T(8,128)(2,1)} %stack.5), calls=%async_computation.3 | async-start | bytes 262144 | tf_op jit(solution)/shard_map/all_to_all | solution.py:51
  210.0 212.5 %all-reduce.3.cloned.1.call-start = ((), (), s32[]{:S(2)}) async-start(), calls=%async_computation.9 | async-start | bytes 7077888 | tf_op jit(solution)/shard_map/psum | solution.py:132
  219.2 49.4 %copy-start.9 = (bf16[64,256]{1,0:T(8,128)(2,1)S(1)}, bf16[64,256]{1,0:T(8,128)(2,1)}, u32[]{:S(2)}) copy-start(bf16[64,256]{1,0:T(8,128)(2,1)} %copy-done.8) | copy-start | bytes 98308
  219.2 49.4 %copy-start.12 = (s32[64,256]{1,0:T(8,128)S(1)}, s32[64,256]{1,0:T(8,128)}, u32[]{:S(2)}) copy-start(s32[64,256]{1,0:T(8,128)} %param.18) | copy-start | bytes 196612
  219.2 49.4 %copy-start.13 = (f32[64,256]{1,0:T(8,128)S(1)}, f32[64,256]{1,0:T(8,128)}, u32[]{:S(2)}) copy-start(f32[64,256]{1,0:T(8,128)} %reduce-scatter.9.cloned.1.call-done) | copy-start | bytes 196612
  219.2 49.4 %copy-start.15 = (bf16[64,256]{1,0:T(8,128)(2,1)S(1)}, bf16[64,256]{1,0:T(8,128)(2,1)}, u32[]{:S(2)}) copy-start(bf16[64,256]{1,0:T(8,128)(2,1)} %param.21) | copy-start | bytes 98308
  221.7 63.4 %copy-start.25 = (s32[128,1]{0,1:T(1,128)S(1)}, s32[128,1]{0,1:T(1,128)}, u32[]{:S(2)}) copy-start(s32[128,1]{0,1:T(1,128)} %copy-done.24) | copy-start | bytes 1540
  221.7 73.3 %copy-start.23 = (pred[128]{0:T(512)(128)(4,1)S(1)}, pred[128]{0:T(512)(128)(4,1)}, u32[]{:S(2)}) copy-start(pred[128]{0:T(512)(128)(4,1)} %get-tuple-element.34) | copy-start | bytes 388
  260.9 8.5 %collective-permute-start.6 = (f32[64,32]{0,1:T(8,128)S(1)}, f32[64,32]{0,1:T(8,128)S(1)}, u32[]{:S(2)}, u32[]{:S(2)}) collective-permute-start(f32[64,32]{0,1:T(8,128)S(1)} %get-tuple-element.43), channel_id=1, source_target_pairs={{0,4},{4,8},{8,12},{12,16},{16,20},{20,24},{24,28},{28,32},{32,36}... | collective-permute-start | bytes 24584 | tf_op jit(solution)/shard_map/ppermute | solution.py:14
  262.8 7.4 %collective-permute-start.7 = (f32[64,32]{0,1:T(8,128)S(1)}, f32[64,32]{0,1:T(8,128)S(1)}, u32[]{:S(2)}, u32[]{:S(2)}) collective-permute-start(f32[64,32]{0,1:T(8,128)S(1)} %get-tuple-element.42), channel_id=1, source_target_pairs={{4,0},{8,4},{12,8},{16,12},{20,16},{24,20},{28,24},{32,28},{36,32}... | collective-permute-start | bytes 24584 | tf_op jit(solution)/shard_map/ppermute | solution.py:17
  271.7 22.6 %all-to-all-start.4 = ((bf16[64,128,2]{0,2,1:T(2,128)(2,1)}), bf16[64,128,2]{0,2,1:T(2,128)(2,1)S(1)}, u32[]{:S(2)}, u32[]{:S(2)}) async-start(bf16[64,128,2]{0,2,1:T(2,128)(2,1)} %bitcast.38), calls=%async_computation.4 | async-start | bytes 131072 | tf_op jit(solution)/shard_map/all_to_all | solution.py:138
  (9 other events, 62.3 us)
Sparse Core Ops, SparseCore 0:
  67.1 23.4 reduce-scatter.6
  117.9 24.9 reduce-scatter.8
  217.7 204.7 all-reduce.2
